TPU v7x, 32 devices: a whole 2x2x4 slice. The times are simulated.
32 devices in a mesh: row: 4 (over z), col: 8 (over y, x, core).
Axes of the slice: x: 2, y: 2, z: 4, core: 2. Of those that a mesh axis runs over, the one named last changes fastest.
Arguments:
- density: float32 [32, 256, 1024], P(None, 'row', 'col'), may hold values from -12 to 12
- active: int32 [4, 64], P('row', 'col'), may hold values from -1 to 7, as said below
- owner_map: int32 [4, 64], P('row', 'col'), may hold values from -1 to 7, as said below
- isovalues: float32 [3], replicated, may hold values from -0.6 to 0.6
Outputs:
- smoothed: float32 [32, 256, 1024], P(None, 'row', 'col')
- crossing: float32 [4, 24, 32768], P('row', 'col')
- normals: float32 [4, 24, 288], P('row', 'col')
Inputs may be any that keep to these rules, and one draw needn't show every extreme that they name: `active`: each device lists distinct numbers of its own 8 bricks, followed by -1 to the end; in each mesh row one device lists all of its 8 bricks and every other device at most 4. `owner_map`: entry t names the mesh column, in the same mesh row, of the owner of the brick at entry t of active, and is -1 exactly where active is -1. At most 1 bricks of one device go to one owner, reached in every mesh row; the owners of a mesh row receive counts that differ by at most one, at most 3, reached in every mesh row.
All inputs are finite; a program needn't handle non-finite values.
Results may differ from a plain program's by a relative error of at most 0.0003.
Values sent between devices are 32-bit elements; how exact they have to be, the bound alone decides.
A program may use at most 256 MiB of HBM per device.

v0:
```python
import functools

import jax
import jax.numpy as jnp
from jax import lax
from jax.experimental import pallas as pl
from jax.experimental.pallas import tpu as pltpu
from jax.sharding import PartitionSpec as P

BRICK = 32
LEVELS = 3
LANES = 128
PAY = 264
CH = 8
MESH = pl.DeviceIdType.MESH
F32 = jnp.float32
DIRS = ((-1, 0), (1, 0), (0, -1), (0, 1), (-1, -1), (-1, 1), (1, -1), (1, 1))


def iota(shape, dim):
    return lax.broadcasted_iota(jnp.int32, shape, dim)


def five(far, near, mid):
    return 10.0 * mid + 4.0 * near - far


def kernel(
    rows_n, cols_n, dens, active, owner, iso,
    smooth, recv,
    dext, side_l, side_r, pack_l, pack_r, shifted, wmat, cells, bricks, nrm, acc, send,
    hs_send, hs_recv, a_send, a_recv,
):
    depth = dens.shape[0]
    height = dens.shape[1]
    ext = height + 16
    r = lax.axis_index("row")
    c = lax.axis_index("col")
    up, down = r > 0, r < rows_n - 1
    left, right = c > 0, c < cols_n - 1

    def exists(dy, dx):
        ok = None
        for d, lo, hi in ((dy, up, down), (dx, left, right)):
            if d:
                e = lo if d < 0 else hi
                ok = e if ok is None else jnp.logical_and(ok, e)
        return ok

    barrier = pltpu.get_barrier_semaphore()
    for dy, dx in DIRS:
        if dy:
            @pl.when(exists(dy, dx))
            def _():
                pl.semaphore_signal(barrier, inc=1, device_id=(r + dy, c + dx), device_id_type=MESH)
    for k in range(1, cols_n):
        pl.semaphore_signal(
            barrier, inc=1, device_id=(r, lax.rem(c + k, cols_n)), device_id_type=MESH
        )

    lane = iota((height, LANES), 1)
    group = lane // 4

    def pack(z, carry):
        first, last = carry
        rolled = pltpu.roll(dens[z], 4 * z, 1)
        first = jnp.where(group == z, rolled, first)
        last = jnp.where(group == (z + depth - 1) % depth, rolled, last)
        dext[z + 2, 8 : 8 + height, :] = dens[z]
        return first, last

    zero = jnp.zeros((height, LANES), F32)
    first, last = lax.fori_loop(0, depth, pack, (zero, zero))
    pack_l[...] = first
    pack_r[...] = last

    n_wait = (cols_n - 1) + (up.astype(jnp.int32) + down.astype(jnp.int32)) * (
        1 + left.astype(jnp.int32) + right.astype(jnp.int32)
    )
    pl.semaphore_wait(barrier, n_wait)

    top, body, bottom = pl.ds(0, 8), pl.ds(8, height), pl.ds(8 + height, 8)
    inner_top, inner_bottom = pl.ds(0, 8), pl.ds(height - 8, 8)
    layers = pl.ds(2, depth)
    plans = {
        (-1, 0): (dens.at[:, inner_top, :], dext.at[layers, bottom, :]),
        (1, 0): (dens.at[:, inner_bottom, :], dext.at[layers, top, :]),
        (0, -1): (pack_l, side_r.at[body, :]),
        (0, 1): (pack_r, side_l.at[body, :]),
        (-1, -1): (pack_l.at[inner_top, :], side_r.at[bottom, :]),
        (-1, 1): (pack_r.at[inner_top, :], side_l.at[bottom, :]),
        (1, -1): (pack_l.at[inner_bottom, :], side_r.at[top, :]),
        (1, 1): (pack_r.at[inner_bottom, :], side_l.at[top, :]),
    }
    halo = []
    for n, (dy, dx) in enumerate(DIRS):
        src, dst = plans[(dy, dx)]
        copy = pltpu.make_async_remote_copy(
            src_ref=src, dst_ref=dst, send_sem=hs_send.at[n], recv_sem=hs_recv.at[n],
            device_id=(r + dy, c + dx), device_id_type=MESH,
        )
        halo.append(copy)

        @pl.when(exists(dy, dx))
        def _():
            copy.start()

    for dy, dx in DIRS:
        @pl.when(jnp.logical_not(exists(-dy, -dx)))
        def _():
            dst = plans[(dy, dx)][1]
            dst[...] = jnp.zeros(dst.shape, F32)
    plane0 = jnp.zeros((ext, LANES), F32)
    for z in (0, 1, depth + 2, depth + 3):
        dext[z] = plane0
    for q in range(4):
        for z in (0, depth + 1, depth + 2):
            shifted[q, z] = plane0

    k_id = iota((2 * LANES, LANES), 0)
    n_id = iota((2 * LANES, LANES), 1)
    k_col = jnp.where(k_id < LANES + LANES // 2, k_id, k_id - 2 * LANES)
    for q in range(4):
        col = n_id + (q - 1)
        gap = jnp.abs(k_col - col)
        tap = jnp.where(gap == 0, 10.0, jnp.where(gap == 1, 4.0, jnp.where(gap == 2, -1.0, 0.0)))
        inside = ((col >= 0) | left) & ((col < LANES) | right)
        wmat[:, q * LANES : (q + 1) * LANES] = jnp.where(
            inside, tap * (1.0 / 4096.0), 0.0
        ).astype(jnp.bfloat16)
    for b in range(2):
        acc[b, LEVELS * 3 * depth * 8 :, :] = jnp.zeros(
            (acc.shape[1] - LEVELS * 3 * depth * 8, LANES), F32
        )

    for n, (dy, dx) in enumerate(DIRS):
        @pl.when(exists(-dy, -dx))
        def _():
            halo[n].wait_recv()
    for n, (dy, dx) in enumerate(DIRS):
        @pl.when(exists(dy, dx))
        def _():
            halo[n].wait_send()

    row_id = iota((ext, LANES), 0)
    lane_id = iota((ext, LANES), 1)
    in_rows = ((row_id >= 8) | up) & ((row_id < 8 + height) | down)

    def along_y(v):
        return five(
            pltpu.roll(v, 2, 0) + pltpu.roll(v, ext - 2, 0),
            pltpu.roll(v, 1, 0) + pltpu.roll(v, ext - 1, 0),
            v,
        )

    def side_filter(v):
        def moved(k):
            if k > 0:
                return jnp.where(lane_id < LANES - 4 * k, pltpu.roll(v, LANES - 4 * k, 1), 0.0)
            return jnp.where(lane_id >= -4 * k, pltpu.roll(v, -4 * k, 1), 0.0)

        out = along_y(five(moved(-2) + moved(2), moved(-1) + moved(1), v))
        return jnp.where(in_rows, out, 0.0)

    side_r[...] = side_filter(side_r[...])
    side_l[...] = pltpu.roll(side_filter(pltpu.roll(side_l[...], 4, 1)), LANES - 4, 1)

    def filtered(z, carry):
        v = [dext[z + i] for i in range(5)]
        main = along_y(five(v[0] + v[4], v[1] + v[3], v[2]))
        main = jnp.where(in_rows, main, 0.0)
        back = (LANES - 4 * z) % LANES
        edge = jnp.where(
            lane_id < 4,
            pltpu.roll(side_r[...], back, 1),
            jnp.where(lane_id >= LANES - 4, pltpu.roll(side_l[...], back, 1), 0.0),
        )
        both = jnp.concatenate([main, edge], axis=1)
        high = both.astype(jnp.bfloat16)
        low = (both - high.astype(F32)).astype(jnp.bfloat16)
        w = wmat[...]
        out = jnp.dot(high, w, preferred_element_type=F32) + jnp.dot(
            low, w, preferred_element_type=F32
        )
        for q in range(4):
            shifted[q, z + 1] = out[:, q * LANES : (q + 1) * LANES]
        smooth[z] = out[8 : 8 + height, LANES : 2 * LANES]
        return carry

    lax.fori_loop(0, depth, filtered, 0)

    levels = [iso[i] for i in range(LEVELS)]

    def layer(z):
        for half in range(2):
            sums = [jnp.zeros((8, LANES), F32)] * (LEVELS * 3)
            for strip in range(4):
                base = 8 + half * BRICK + strip * 8

                def at(q, dz=0, dy=0):
                    return shifted[q, z + 1 + dz, pl.ds(base + dy, 8), :]

                here, ahead_x = at(1), at(2)
                ahead_y, ahead_z = at(1, 0, 1), at(1, 1)
                back_z = at(1, -1)
                grads = (
                    (
                        ahead_z - back_z,
                        at(2, 1) - at(2, -1),
                        at(1, 1, 1) - at(1, -1, 1),
                        at(1, 2) - here,
                    ),
                    (
                        ahead_y - at(1, 0, -1),
                        at(2, 0, 1) - at(2, 0, -1),
                        at(1, 0, 2) - here,
                        at(1, 1, 1) - at(1, 1, -1),
                    ),
                    (
                        ahead_x - at(0),
                        at(3) - here,
                        at(2, 0, 1) - at(0, 0, 1),
                        at(2, 1) - at(0, 1),
                    ),
                )
                crossing = jnp.zeros((8, LANES), F32)
                for i in range(LEVELS):
                    minus = levels[i] - here
                    size = jnp.abs(minus)
                    own = None
                    terms = []
                    for ahead in (ahead_x, ahead_y, ahead_z):
                        upper = ahead - levels[i]
                        w = jnp.maximum(0.0, minus * upper)
                        crossing = crossing + w
                        part = w * jnp.abs(upper)
                        own = part if own is None else own + part
                        terms.append(w * size)
                    for m in range(3):
                        g = grads[m]
                        sums[i * 3 + m] = sums[i * 3 + m] + (
                            (own * g[0] + terms[0] * g[1]) + (terms[1] * g[2] + terms[2] * g[3])
                        )
                cells[half * BRICK + strip * 8 : half * BRICK + strip * 8 + 8, :] = crossing
            for n in range(LEVELS * 3):
                acc[half, pl.ds(pl.multiple_of((n * depth + z) * 8, 8), 8), :] = sums[n]
        quad = iota((height // 4, LANES), 1) // BRICK
        t = [cells[pl.ds(b, height // 4, stride=4), :] for b in range(4)]
        u = [None] * 4
        for b in range(2):
            u[b] = jnp.where(quad < 2, t[b], pltpu.roll(t[b + 2], 64, 1))
            u[b + 2] = jnp.where(quad < 2, pltpu.roll(t[b], 64, 1), t[b + 2])
        even = quad % 2 == 0
        for b in (0, 2):
            o0 = jnp.where(even, u[b], pltpu.roll(u[b + 1], 32, 1))
            o1 = jnp.where(even, pltpu.roll(u[b], 96, 1), u[b + 1])
            for half in range(2):
                at_rows = pl.ds(pl.multiple_of(z * 8, 8), 8)
                bricks[half * 4 + b, at_rows, :] = o0[half * 8 : half * 8 + 8]
                bricks[half * 4 + b + 1, at_rows, :] = o1[half * 8 : half * 8 + 8]

    picks = []
    for k in range(cols_n):
        target = lax.rem(c + k, cols_n)
        brick = jnp.int32(0)
        found = jnp.int32(0)
        for t in range(active.shape[1]):
            hit = jnp.logical_and(owner[0, t] == target, active[0, t] >= 0)
            brick = jnp.where(hit, active[0, t], brick)
            found = jnp.where(hit, 1, found)
        picks.append((brick, found))

    def copy_of(k, chunk, start, count):
        rows = pl.ds(start, count)
        return pltpu.make_async_remote_copy(
            src_ref=send.at[k, rows, :], dst_ref=recv.at[c, rows, :],
            send_sem=a_send.at[k, chunk], recv_sem=a_recv.at[k, chunk],
            device_id=(r, lax.rem(c + k, cols_n)), device_id_type=MESH,
        )

    chunks = depth // CH
    crows = CH * 8

    def one_chunk(chunk, carry):
        def one_layer(z, inner):
            layer(chunk * CH + z)
            return inner

        lax.fori_loop(0, CH, one_layer, 0)
        start = pl.multiple_of(chunk * crows, crows)
        rows = pl.ds(start, crows)
        for k in range(1, cols_n):
            send[k, rows, :] = bricks[picks[k][0], rows, :]
            copy_of(k, chunk, start, crows).start()
        recv[c, rows, :] = bricks[picks[0][0], rows, :]
        return carry

    lax.fori_loop(0, chunks, one_chunk, 0)

    pick = (iota((8, LANES), 1) // BRICK == iota((8, LANES), 0)).astype(F32)
    wide = acc.shape[1] // 8
    for half in range(2):
        total = acc[half, pl.ds(0, wide, stride=8), :]
        for s in range(1, 8):
            total = total + acc[half, pl.ds(s, wide, stride=8), :]
        out = lax.dot_general(
            pick, total, (((1,), (1,)), ((), ())),
            precision=lax.Precision.HIGHEST, preferred_element_type=F32,
        ) * (1.0 / 32.0)
        for b in range(4):
            for part in range(wide // LANES):
                nrm[half * 4 + b, part : part + 1, :] = out[
                    b : b + 1, part * LANES : (part + 1) * LANES
                ]
    flag_row = iota((8, LANES), 0) == 3
    base = chunks * crows
    for k in range(cols_n):
        brick, found = picks[k]
        tail = jnp.where(flag_row, found.astype(F32), nrm[brick])
        if k:
            send[k, base : base + 8, :] = tail
            copy_of(k, chunks, base, 8).start()
        else:
            recv[c, base : base + 8, :] = tail

    for k in range(1, cols_n):
        for chunk in range(chunks):
            copy_of(k, chunk, chunk * crows, crows).wait()
        copy_of(k, chunks, base, 8).wait()


def place(recv, crossing, normals):
    sources = recv.shape[0]
    rows = recv.shape[1] - 8
    slots = crossing.shape[1]
    count = jnp.int32(0)
    index = [jnp.int32(0)] * slots
    filled = [jnp.int32(0)] * slots
    for s in range(sources):
        flag = jnp.max(recv[s, rows + 3 : rows + 4, :]) > 0.5
        for n in range(slots):
            hit = jnp.logical_and(flag, count == n)
            index[n] = jnp.where(hit, s, index[n])
            filled[n] = jnp.where(hit, 1, filled[n])
        count = count + flag.astype(jnp.int32)

    def block(i, carry):
        start = pl.multiple_of(i * 8, 8)
        for n in range(slots):
            v = recv[index[n], pl.ds(start, 8), :]
            v = jnp.where(filled[n] > 0, v, 0.0)
            for s in range(8):
                at = pl.ds(pl.multiple_of((start + s) * LANES, LANES), LANES)
                crossing[0, n : n + 1, at] = v[s : s + 1, :]
        return carry

    lax.fori_loop(0, rows // 8, block, 0)
    for n in range(slots):
        v = jnp.where(filled[n] > 0, recv[index[n], rows : rows + 8, :], 0.0)
        length = normals.shape[2]
        for p in range(0, length, LANES):
            width = min(LANES, length - p)
            normals[0, n : n + 1, p : p + width] = v[p // LANES : p // LANES + 1, :width]


def shards(rows_n, cols_n, density, active, owner_map, isovalues):
    depth, height, width = density.shape
    ext = height + 16
    local = active.shape[1]
    chunks = depth // CH
    vmem = pl.BlockSpec(memory_space=pltpu.VMEM)
    smem = pl.BlockSpec(memory_space=pltpu.SMEM)
    smoothed, received = pl.pallas_call(
        functools.partial(kernel, rows_n, cols_n),
        out_shape=(
            jax.ShapeDtypeStruct(density.shape, F32),
            jax.ShapeDtypeStruct((cols_n, PAY, LANES), F32),
        ),
        in_specs=[vmem, smem, smem, smem],
        out_specs=(vmem, vmem),
        scratch_shapes=[
            pltpu.VMEM((depth + 4, ext, LANES), F32),
            pltpu.VMEM((ext, LANES), F32),
            pltpu.VMEM((ext, LANES), F32),
            pltpu.VMEM((height, LANES), F32),
            pltpu.VMEM((height, LANES), F32),
            pltpu.VMEM((4, depth + 3, ext, LANES), F32),
            pltpu.VMEM((2 * LANES, 4 * LANES), jnp.bfloat16),
            pltpu.VMEM((height, LANES), F32),
            pltpu.VMEM((local, depth * 8, LANES), F32),
            pltpu.VMEM((local, 8, LANES), F32),
            pltpu.VMEM((2, 384 * 8, LANES), F32),
            pltpu.VMEM((cols_n, PAY, LANES), F32),
            pltpu.SemaphoreType.DMA((8,)),
            pltpu.SemaphoreType.DMA((8,)),
            pltpu.SemaphoreType.DMA((cols_n, chunks + 1)),
            pltpu.SemaphoreType.DMA((cols_n, chunks + 1)),
        ],
        compiler_params=pltpu.CompilerParams(
            collective_id=0, has_side_effects=True, vmem_limit_bytes=48 << 20
        ),
        name="halo_surface_exchange",
    )(density, active, owner_map, isovalues)
    quarter = local // 4
    capacity = (local + (cols_n - 1) * quarter + cols_n - 1) // cols_n
    crossing, normals = pl.pallas_call(
        place,
        out_shape=(
            jax.ShapeDtypeStruct((1, capacity, depth * BRICK * BRICK), F32),
            jax.ShapeDtypeStruct((1, capacity, LEVELS * 3 * depth), F32),
        ),
        in_specs=[vmem],
        out_specs=(vmem, vmem),
        compiler_params=pltpu.CompilerParams(vmem_limit_bytes=32 << 20),
        name="place_slots",
    )(received)
    return smoothed, crossing, normals


def solution(mesh):
    placed = (P(None, "row", "col"), P("row", "col"), P("row", "col"), P())
    return jax.shard_map(
        functools.partial(shards, mesh.shape["row"], mesh.shape["col"]),
        mesh=mesh,
        in_specs=placed,
        out_specs=(P(None, "row", "col"), P("row", "col", None), P("row", "col", None)),
        check_vma=False,
    )
```

profile of v0, /device:TPU:0, one launch (start us, length us, event | category | flops | bytes accessed | tf_op | source)
XLA Modules:
  0.0 44.3 jit_solution(12886795697140644903)
XLA Ops:
  0.6 0.0 copy-start
  0.6 1.2 %copy-done = f32[32,64,128]{2,1,0:T(8,128)S(1)} copy-done((f32[32,64,128]{2,1,0:T(8,128)S(1)}, f32[32,64,128]{2,1,0:T(8,128)}, u32[]{:S(2)}) %copy-start) | copy-done | bytes 1048600
  1.9 0.0 copy-start.1
  1.9 0.7 %copy-done.1 = s32[1,8]{1,0:T(1,128)S(1)} copy-done((s32[1,8]{1,0:T(1,128)S(1)}, s32[1,8]{1,0:T(1,128)}, u32[]{:S(2)}) %copy-start.1) | copy-done | bytes 56
  2.5 0.0 copy-start.2
  2.5 0.7 %copy-done.2 = s32[1,8]{1,0:T(1,128)S(1)} copy-done((s32[1,8]{1,0:T(1,128)S(1)}, s32[1,8]{1,0:T(1,128)}, u32[]{:S(2)}) %copy-start.2) | copy-done | bytes 56
  3.2 0.0 copy-start.3
  3.2 0.7 %copy-done.3 = f32[3]{0:T(128)S(1)} copy-done((f32[3]{0:T(128)S(1)}, f32[3]{0:T(128)}, u32[]{:S(2)}) %copy-start.3) | copy-done | bytes 36
  3.8 36.8 %halo_surface_exchange.1 = (f32[32,64,128]{2,1,0:T(8,128)S(1)}, f32[8,264,128]{2,1,0:T(8,128)S(1)}) custom-call(f32[32,64,128]{2,1,0:T(8,128)S(1)} %copy-done, s32[1,8]{1,0:T(1,128)S(1)} %copy-done.1, s32[1,8]{1,0:T(1,128)S(1)} %copy-done.2, f32[3]{0:T(128)S(1)} %copy-done.3), custom_call_target="tpu_custom_call" | custom-call | tf_op jit(solution)/shard_map/halo_surface_exchange/pallas_call | solution.py:373
  40.6 1.0 %place_slots.1 = (f32[1,3,32768]{2,1,0:T(4,128)S(1)}, f32[1,3,288]{2,1,0:T(4,128)S(1)}) custom-call(f32[8,264,128]{2,1,0:T(8,128)S(1)} %get-tuple-element.8.recv), custom_call_target="tpu_custom_call" | custom-call | tf_op jit(solution)/shard_map/place_slots/pallas_call | solution.py:406
  41.6 1.2 %copy.7 = f32[1,3,32768]{2,0,1:T(1,128)} copy(f32[1,3,32768]{2,1,0:T(4,128)S(1)} %get-tuple-element.12) | data formatting | bytes 786432
  42.7 0.6 %copy.8 = f32[1,3,288]{2,0,1:T(1,128)} copy(f32[1,3,288]{2,1,0:T(4,128)S(1)} %get-tuple-element.13) | data formatting | bytes 6912
  43.3 1.0 %copy.10 = f32[32,64,128]{2,1,0:T(8,128)} copy(f32[32,64,128]{2,1,0:T(8,128)S(1)} %get-tuple-element.17) | data formatting | bytes 2097152
Async XLA Ops:
  0.6 1.2 %copy-start = (f32[32,64,128]{2,1,0:T(8,128)S(1)}, f32[32,64,128]{2,1,0:T(8,128)}, u32[]{:S(2)}) copy-start(f32[32,64,128]{2,1,0:T(8,128)} %dens.1) | copy-start | bytes 3145732
  1.9 0.7 %copy-start.1 = (s32[1,8]{1,0:T(1,128)S(1)}, s32[1,8]{1,0:T(1,128)}, u32[]{:S(2)}) copy-start(s32[1,8]{1,0:T(1,128)} %active.1) | copy-start | bytes 100
  2.5 0.7 %copy-start.2 = (s32[1,8]{1,0:T(1,128)S(1)}, s32[1,8]{1,0:T(1,128)}, u32[]{:S(2)}) copy-start(s32[1,8]{1,0:T(1,128)} %owner.1) | copy-start | bytes 100
  3.2 0.7 %copy-start.3 = (f32[3]{0:T(128)S(1)}, f32[3]{0:T(128)}, u32[]{:S(2)}) copy-start(f32[3]{0:T(128)} %iso.1) | copy-start | bytes 40
where the time goes:
time: 44.5 us; the launch traced here: 44.3 us
  Pallas kernels  37.7 us (85%)
  local copies, waits for them, and re-layouts  5.9 us (13%)
  between operations  0.66 us (1%)
    pallas_call x1, Pallas kernels, shards(): pl.pallas_call(functools.partial(kernel, rows_n, cols_n), out_shape=(jax....  36.8 us
    unnamed x11, local copies, waits for them, and re-layouts  5.9 us
    pallas_call x1, Pallas kernels, shards(): pl.pallas_call(place, out_shape=(jax.ShapeDtypeStruct((1, capacity, depth...  0.96 us

commit v1 on v0

--- a/solution.py
+++ b/solution.py
@@ -11,7 +11,7 @@
 LEVELS = 3
 LANES = 128
 PAY = 264
-CH = 8
+CH = 4
 MESH = pl.DeviceIdType.MESH
 F32 = jnp.float32
 DIRS = ((-1, 0), (1, 0), (0, -1), (0, 1), (-1, -1), (-1, 1), (1, -1), (1, 1))
@@ -26,10 +26,11 @@
 
 
 def kernel(
-    rows_n, cols_n, dens, active, owner, iso,
+    rows_n, cols_n, dens, active_in, owner_in, iso_in,
     smooth, recv,
-    dext, side_l, side_r, pack_l, pack_r, shifted, wmat, cells, bricks, nrm, acc, send,
-    hs_send, hs_recv, a_send, a_recv,
+    dext, side_l, side_r, pack_l, pack_r, pack_y, side_y, shifted, wmat, lhs, cells, bricks, nrm,
+    acc, send, active, owner, iso,
+    in_sem, hs_send, hs_recv, a_send, a_recv,
 ):
     depth = dens.shape[0]
     height = dens.shape[1]
@@ -47,6 +48,20 @@
                 ok = e if ok is None else jnp.logical_and(ok, e)
         return ok
 
+    layers = pl.ds(2, depth)
+    loads = [
+        pltpu.make_async_copy(src, dst, in_sem.at[n])
+        for n, (src, dst) in enumerate(
+            (
+                (dens, dext.at[layers, pl.ds(8, height), :]),
+                (active_in, active),
+                (owner_in, owner),
+                (iso_in, iso),
+            )
+        )
+    ]
+    for load in loads:
+        load.start()
     barrier = pltpu.get_barrier_semaphore()
     for dy, dx in DIRS:
         if dy:
@@ -63,14 +78,30 @@
 
     def pack(z, carry):
         first, last = carry
-        rolled = pltpu.roll(dens[z], 4 * z, 1)
+        rolled = pltpu.roll(dext[z + 2, 8 : 8 + height, :], 4 * z, 1)
         first = jnp.where(group == z, rolled, first)
         last = jnp.where(group == (z + depth - 1) % depth, rolled, last)
-        dext[z + 2, 8 : 8 + height, :] = dens[z]
         return first, last
 
+    upper_half = iota((8, LANES), 0) < 4
+
+    def pack_rows(pair, carry):
+        z = 2 * pair + 2
+        at_rows = pl.ds(pl.multiple_of(pair * 8, 8), 8)
+        pack_y[0, at_rows, :] = jnp.where(
+            upper_half, dext[z, 8:16, :], pltpu.roll(dext[z + 1, 8:16, :], 4, 0)
+        )
+        pack_y[1, at_rows, :] = jnp.where(
+            upper_half,
+            pltpu.roll(dext[z, height : height + 8, :], 4, 0),
+            dext[z + 1, height : height + 8, :],
+        )
+        return carry
+
     zero = jnp.zeros((height, LANES), F32)
-    first, last = lax.fori_loop(0, depth, pack, (zero, zero))
+    loads[0].wait()
+    lax.fori_loop(0, depth // 2, pack_rows, 0, unroll=4)
+    first, last = lax.fori_loop(0, depth, pack, (zero, zero), unroll=4)
     pack_l[...] = first
     pack_r[...] = last
 
@@ -81,10 +112,9 @@
 
     top, body, bottom = pl.ds(0, 8), pl.ds(8, height), pl.ds(8 + height, 8)
     inner_top, inner_bottom = pl.ds(0, 8), pl.ds(height - 8, 8)
-    layers = pl.ds(2, depth)
     plans = {
-        (-1, 0): (dens.at[:, inner_top, :], dext.at[layers, bottom, :]),
-        (1, 0): (dens.at[:, inner_bottom, :], dext.at[layers, top, :]),
+        (-1, 0): (pack_y.at[0], side_y.at[1]),
+        (1, 0): (pack_y.at[1], side_y.at[0]),
         (0, -1): (pack_l, side_r.at[body, :]),
         (0, 1): (pack_r, side_l.at[body, :]),
         (-1, -1): (pack_l.at[inner_top, :], side_r.at[bottom, :]),
@@ -125,9 +155,9 @@
         gap = jnp.abs(k_col - col)
         tap = jnp.where(gap == 0, 10.0, jnp.where(gap == 1, 4.0, jnp.where(gap == 2, -1.0, 0.0)))
         inside = ((col >= 0) | left) & ((col < LANES) | right)
-        wmat[:, q * LANES : (q + 1) * LANES] = jnp.where(
-            inside, tap * (1.0 / 4096.0), 0.0
-        ).astype(jnp.bfloat16)
+        band = jnp.where(inside, tap * (1.0 / 4096.0), 0.0).astype(jnp.bfloat16)
+        for part in range(2):
+            wmat[part * 2 * LANES : (part + 1) * 2 * LANES, q * LANES : (q + 1) * LANES] = band
     for b in range(2):
         acc[b, LEVELS * 3 * depth * 8 :, :] = jnp.zeros(
             (acc.shape[1] - LEVELS * 3 * depth * 8, LANES), F32
@@ -137,10 +167,20 @@
         @pl.when(exists(-dy, -dx))
         def _():
             halo[n].wait_recv()
-    for n, (dy, dx) in enumerate(DIRS):
-        @pl.when(exists(dy, dx))
-        def _():
-            halo[n].wait_send()
+    for load in loads[1:]:
+        load.wait()
+
+    def unpack_rows(pair, carry):
+        z = 2 * pair + 2
+        at_rows = pl.ds(pl.multiple_of(pair * 8, 8), 8)
+        above, below = side_y[0, at_rows, :], side_y[1, at_rows, :]
+        dext[z, 0:8, :] = pltpu.roll(above, 4, 0)
+        dext[z + 1, 0:8, :] = above
+        dext[z, 8 + height :, :] = below
+        dext[z + 1, 8 + height :, :] = pltpu.roll(below, 4, 0)
+        return carry
+
+    lax.fori_loop(0, depth // 2, unpack_rows, 0, unroll=4)
 
     row_id = iota((ext, LANES), 0)
     lane_id = iota((ext, LANES), 1)
@@ -165,29 +205,30 @@
     side_r[...] = side_filter(side_r[...])
     side_l[...] = pltpu.roll(side_filter(pltpu.roll(side_l[...], 4, 1)), LANES - 4, 1)
 
-    def filtered(z, carry):
-        v = [dext[z + i] for i in range(5)]
-        main = along_y(five(v[0] + v[4], v[1] + v[3], v[2]))
-        main = jnp.where(in_rows, main, 0.0)
-        back = (LANES - 4 * z) % LANES
-        edge = jnp.where(
-            lane_id < 4,
-            pltpu.roll(side_r[...], back, 1),
-            jnp.where(lane_id >= LANES - 4, pltpu.roll(side_l[...], back, 1), 0.0),
-        )
-        both = jnp.concatenate([main, edge], axis=1)
-        high = both.astype(jnp.bfloat16)
-        low = (both - high.astype(F32)).astype(jnp.bfloat16)
-        w = wmat[...]
-        out = jnp.dot(high, w, preferred_element_type=F32) + jnp.dot(
-            low, w, preferred_element_type=F32
-        )
-        for q in range(4):
-            shifted[q, z + 1] = out[:, q * LANES : (q + 1) * LANES]
-        smooth[z] = out[8 : 8 + height, LANES : 2 * LANES]
-        return carry
-
-    lax.fori_loop(0, depth, filtered, 0)
+    def filter_chunk(chunk):
+        for i in range(CH):
+            z = chunk * CH + i
+            v = [dext[z + n] for n in range(5)]
+            main = along_y(five(v[0] + v[4], v[1] + v[3], v[2]))
+            main = jnp.where(in_rows, main, 0.0)
+            back = (LANES - 4 * z) % LANES
+            edge = jnp.where(
+                lane_id < 4,
+                pltpu.roll(side_r[...], back, 1),
+                jnp.where(lane_id >= LANES - 4, pltpu.roll(side_l[...], back, 1), 0.0),
+            )
+            for n, part in enumerate((main, edge)):
+                high = part.astype(jnp.bfloat16)
+                low = (part - high.astype(F32)).astype(jnp.bfloat16)
+                rows = slice(i * ext, (i + 1) * ext)
+                lhs[rows, n * LANES : (n + 1) * LANES] = high
+                lhs[rows, (n + 2) * LANES : (n + 3) * LANES] = low
+        out = jnp.dot(lhs[...], wmat[...], preferred_element_type=F32)
+        for i in range(CH):
+            z = chunk * CH + i
+            for q in range(4):
+                shifted[q, z + 1] = out[i * ext : (i + 1) * ext, q * LANES : (q + 1) * LANES]
+            smooth[z] = out[i * ext + 8 : i * ext + 8 + height, LANES : 2 * LANES]
 
     levels = [iso[i] for i in range(LEVELS)]
 
@@ -282,11 +323,15 @@
     crows = CH * 8
 
     def one_chunk(chunk, carry):
+        @pl.when(chunk + 1 < chunks)
+        def _():
+            filter_chunk(chunk + 1)
+
         def one_layer(z, inner):
             layer(chunk * CH + z)
             return inner
 
-        lax.fori_loop(0, CH, one_layer, 0)
+        lax.fori_loop(0, CH, one_layer, 0, unroll=2)
         start = pl.multiple_of(chunk * crows, crows)
         rows = pl.ds(start, crows)
         for k in range(1, cols_n):
@@ -295,6 +340,7 @@
         recv[c, rows, :] = bricks[picks[0][0], rows, :]
         return carry
 
+    filter_chunk(0)
     lax.fori_loop(0, chunks, one_chunk, 0)
 
     pick = (iota((8, LANES), 1) // BRICK == iota((8, LANES), 0)).astype(F32)
@@ -327,12 +373,19 @@
         for chunk in range(chunks):
             copy_of(k, chunk, chunk * crows, crows).wait()
         copy_of(k, chunks, base, 8).wait()
-
-
-def place(recv, crossing, normals):
+    for n, (dy, dx) in enumerate(DIRS):
+        @pl.when(exists(dy, dx))
+        def _():
+            halo[n].wait_send()
+
+
+def place(smooth_in, recv, smooth, crossing, normals, empty, vectors, sems):
+    keep = pltpu.make_async_copy(smooth_in, smooth, sems.at[0])
+    keep.start()
     sources = recv.shape[0]
     rows = recv.shape[1] - 8
-    slots = crossing.shape[1]
+    slots = crossing.shape[0]
+    empty[...] = jnp.zeros(empty.shape, F32)
     count = jnp.int32(0)
     index = [jnp.int32(0)] * slots
     filled = [jnp.int32(0)] * slots
@@ -343,24 +396,27 @@
             index[n] = jnp.where(hit, s, index[n])
             filled[n] = jnp.where(hit, 1, filled[n])
         count = count + flag.astype(jnp.int32)
-
-    def block(i, carry):
-        start = pl.multiple_of(i * 8, 8)
-        for n in range(slots):
-            v = recv[index[n], pl.ds(start, 8), :]
-            v = jnp.where(filled[n] > 0, v, 0.0)
-            for s in range(8):
-                at = pl.ds(pl.multiple_of((start + s) * LANES, LANES), LANES)
-                crossing[0, n : n + 1, at] = v[s : s + 1, :]
-        return carry
-
-    lax.fori_loop(0, rows // 8, block, 0)
+    copies = []
+    for n in range(slots):
+        copy = pltpu.make_async_copy(
+            recv.at[index[n], pl.ds(0, rows), :], crossing.at[n], sems.at[2 + n]
+        )
+        none = pltpu.make_async_copy(empty, crossing.at[n], sems.at[2 + n])
+        copies.append(none)
+        pl.when(filled[n] > 0)(copy.start)
+        pl.when(filled[n] == 0)(none.start)
+    length = normals.shape[2]
     for n in range(slots):
         v = jnp.where(filled[n] > 0, recv[index[n], rows : rows + 8, :], 0.0)
-        length = normals.shape[2]
         for p in range(0, length, LANES):
             width = min(LANES, length - p)
-            normals[0, n : n + 1, p : p + width] = v[p // LANES : p // LANES + 1, :width]
+            vectors[n, :, p : p + width] = v[p // LANES : p // LANES + 1, :width]
+    last = pltpu.make_async_copy(vectors, normals, sems.at[1])
+    last.start()
+    for copy in copies:
+        copy.wait()
+    last.wait()
+    keep.wait()
 
 
 def shards(rows_n, cols_n, density, active, owner_map, isovalues):
@@ -369,14 +425,15 @@
     local = active.shape[1]
     chunks = depth // CH
     vmem = pl.BlockSpec(memory_space=pltpu.VMEM)
-    smem = pl.BlockSpec(memory_space=pltpu.SMEM)
+    hbm = pl.BlockSpec(memory_space=pltpu.HBM)
+    anywhere = pl.BlockSpec(memory_space=pl.ANY)
     smoothed, received = pl.pallas_call(
         functools.partial(kernel, rows_n, cols_n),
         out_shape=(
             jax.ShapeDtypeStruct(density.shape, F32),
             jax.ShapeDtypeStruct((cols_n, PAY, LANES), F32),
         ),
-        in_specs=[vmem, smem, smem, smem],
+        in_specs=[hbm] * 4,
         out_specs=(vmem, vmem),
         scratch_shapes=[
             pltpu.VMEM((depth + 4, ext, LANES), F32),
@@ -384,13 +441,20 @@
             pltpu.VMEM((ext, LANES), F32),
             pltpu.VMEM((height, LANES), F32),
             pltpu.VMEM((height, LANES), F32),
+            pltpu.VMEM((2, 4 * depth, LANES), F32),
+            pltpu.VMEM((2, 4 * depth, LANES), F32),
             pltpu.VMEM((4, depth + 3, ext, LANES), F32),
-            pltpu.VMEM((2 * LANES, 4 * LANES), jnp.bfloat16),
+            pltpu.VMEM((4 * LANES, 4 * LANES), jnp.bfloat16),
+            pltpu.VMEM((CH * ext, 4 * LANES), jnp.bfloat16),
             pltpu.VMEM((height, LANES), F32),
             pltpu.VMEM((local, depth * 8, LANES), F32),
             pltpu.VMEM((local, 8, LANES), F32),
             pltpu.VMEM((2, 384 * 8, LANES), F32),
             pltpu.VMEM((cols_n, PAY, LANES), F32),
+            pltpu.SMEM(active.shape, jnp.int32),
+            pltpu.SMEM(owner_map.shape, jnp.int32),
+            pltpu.SMEM(isovalues.shape, F32),
+            pltpu.SemaphoreType.DMA((4,)),
             pltpu.SemaphoreType.DMA((8,)),
             pltpu.SemaphoreType.DMA((8,)),
             pltpu.SemaphoreType.DMA((cols_n, chunks + 1)),
@@ -403,18 +467,26 @@
     )(density, active, owner_map, isovalues)
     quarter = local // 4
     capacity = (local + (cols_n - 1) * quarter + cols_n - 1) // cols_n
-    crossing, normals = pl.pallas_call(
+    cells = depth * BRICK * BRICK
+    length = LEVELS * 3 * depth
+    smoothed, crossing, normals = pl.pallas_call(
         place,
         out_shape=(
-            jax.ShapeDtypeStruct((1, capacity, depth * BRICK * BRICK), F32),
-            jax.ShapeDtypeStruct((1, capacity, LEVELS * 3 * depth), F32),
+            jax.ShapeDtypeStruct(density.shape, F32),
+            jax.ShapeDtypeStruct((capacity, cells // LANES, LANES), F32),
+            jax.ShapeDtypeStruct((capacity, 1, length), F32),
         ),
-        in_specs=[vmem],
-        out_specs=(vmem, vmem),
+        in_specs=[anywhere, vmem],
+        out_specs=(hbm, hbm, hbm),
+        scratch_shapes=[
+            pltpu.VMEM((cells // LANES, LANES), F32),
+            pltpu.VMEM((capacity, 1, length), F32),
+            pltpu.SemaphoreType.DMA((2 + capacity,)),
+        ],
         compiler_params=pltpu.CompilerParams(vmem_limit_bytes=32 << 20),
         name="place_slots",
-    )(received)
-    return smoothed, crossing, normals
+    )(smoothed, received)
+    return smoothed, crossing.reshape(1, capacity, cells), normals.reshape(1, capacity, length)
 
 
 def solution(mesh):

time: 44.5 us -> 31.8 us (0.71)
  Pallas kernels: 37.7 us -> 27.8 us
  local copies, waits for them, and re-layouts: 5.9 us -> 3.18 us
    pallas_call x1, Pallas kernels: 36.8 us -> 26.6 us  [shards(): pl.pallas_call(functools.partial(kernel, rows_n, cols_n), out_shape=(jax....]
    unnamed x11 -> x8, local copies, waits for them, and re-layouts: 5.9 us -> 3.18 us
where the time goes in v1:
time: 31.8 us; the launch traced here: 31.6 us
  Pallas kernels  27.8 us (87%)
  local copies, waits for them, and re-layouts  3.18 us (10%)
  between operations  0.65 us (2%)
    pallas_call x1, Pallas kernels, shards(): pl.pallas_call(functools.partial(kernel, rows_n, cols_n), out_shape=(jax....  26.6 us
    unnamed x8, local copies, waits for them, and re-layouts  3.18 us
    pallas_call x1, Pallas kernels, shards(): pl.pallas_call(place, out_shape=(jax.ShapeDtypeStruct(density.shape, F32)...  1.14 us

profile of v1, /device:TPU:0, one launch (start us, length us, event | category | flops | bytes accessed | tf_op | source)
XLA Modules:
  0.0 31.6 jit_solution(2163839120214524022)
XLA Ops:
  0.6 0.0 copy-start
  0.6 1.2 %copy-done = f32[32,64,128]{2,1,0:T(8,128)S(1)} copy-done((f32[32,64,128]{2,1,0:T(8,128)S(1)}, f32[32,64,128]{2,1,0:T(8,128)}, u32[]{:S(2)}) %copy-start) | copy-done | bytes 1048600
  1.9 0.0 copy-start.1
  1.9 0.7 %copy-done.1 = s32[1,8]{1,0:T(1,128)S(1)} copy-done((s32[1,8]{1,0:T(1,128)S(1)}, s32[1,8]{1,0:T(1,128)}, u32[]{:S(2)}) %copy-start.1) | copy-done | bytes 56
  2.5 0.0 copy-start.2
  2.5 0.7 %copy-done.2 = s32[1,8]{1,0:T(1,128)S(1)} copy-done((s32[1,8]{1,0:T(1,128)S(1)}, s32[1,8]{1,0:T(1,128)}, u32[]{:S(2)}) %copy-start.2) | copy-done | bytes 56
  3.2 0.0 copy-start.3
  3.2 0.7 %copy-done.3 = f32[3]{0:T(128)S(1)} copy-done((f32[3]{0:T(128)S(1)}, f32[3]{0:T(128)}, u32[]{:S(2)}) %copy-start.3) | copy-done | bytes 36
  3.8 26.6 %halo_surface_exchange.1 = (f32[32,64,128]{2,1,0:T(8,128)S(1)}, f32[8,264,128]{2,1,0:T(8,128)S(1)}) custom-call(f32[32,64,128]{2,1,0:T(8,128)S(1)} %copy-done, s32[1,8]{1,0:T(1,128)S(1)} %copy-done.1, s32[1,8]{1,0:T(1,128)S(1)} %copy-done.2, f32[3]{0:T(128)S(1)} %copy-done.3), custom_call_target="tpu_custom_call" | custom-call | tf_op jit(solution)/shard_map/halo_surface_exchange/pallas_call | solution.py:430
  30.5 1.1 %place_slots.1 = (f32[32,64,128]{2,1,0:T(8,128)}, f32[3,256,128]{2,1,0:T(8,128)}, f32[3,1,288]{2,1,0:T(1,128)}) custom-call(f32[32,64,128]{2,1,0:T(8,128)S(1)} %get-tuple-element.8.smooth_in, f32[8,264,128]{2,1,0:T(8,128)S(1)} %get-tuple-element.9.recv), custom_call_target="tpu_custom_call" | custom-call | tf_op jit(solution)/shard_map/place_slots/pallas_call | solution.py:472
Async XLA Ops:
  0.6 1.2 %copy-start = (f32[32,64,128]{2,1,0:T(8,128)S(1)}, f32[32,64,128]{2,1,0:T(8,128)}, u32[]{:S(2)}) copy-start(f32[32,64,128]{2,1,0:T(8,128)} %dens.1) | copy-start | bytes 3145732
  1.9 0.7 %copy-start.1 = (s32[1,8]{1,0:T(1,128)S(1)}, s32[1,8]{1,0:T(1,128)}, u32[]{:S(2)}) copy-start(s32[1,8]{1,0:T(1,128)} %active_in.1) | copy-start | bytes 100
  2.5 0.7 %copy-start.2 = (s32[1,8]{1,0:T(1,128)S(1)}, s32[1,8]{1,0:T(1,128)}, u32[]{:S(2)}) copy-start(s32[1,8]{1,0:T(1,128)} %owner_in.1) | copy-start | bytes 100
  3.2 0.7 %copy-start.3 = (f32[3]{0:T(128)S(1)}, f32[3]{0:T(128)}, u32[]{:S(2)}) copy-start(f32[3]{0:T(128)} %iso_in.1) | copy-start | bytes 40

commit v2 on v1

--- a/solution.py
+++ b/solution.py
@@ -26,10 +26,10 @@
 
 
 def kernel(
-    rows_n, cols_n, dens, active_in, owner_in, iso_in,
+    rows_n, cols_n, dens, codes_in, iso_in,
     smooth, recv,
     dext, side_l, side_r, pack_l, pack_r, pack_y, side_y, shifted, wmat, lhs, cells, bricks, nrm,
-    acc, send, active, owner, iso,
+    acc, send, inner, codes, iso,
     in_sem, hs_send, hs_recv, a_send, a_recv,
 ):
     depth = dens.shape[0]
@@ -54,8 +54,7 @@
         for n, (src, dst) in enumerate(
             (
                 (dens, dext.at[layers, pl.ds(8, height), :]),
-                (active_in, active),
-                (owner_in, owner),
+                (codes_in, codes),
                 (iso_in, iso),
             )
         )
@@ -163,6 +162,16 @@
             (acc.shape[1] - LEVELS * 3 * depth * 8, LANES), F32
         )
 
+    def along_z(z, start, stop):
+        v = [dext[z + n, start:stop, :] for n in range(5)]
+        return five(v[0] + v[4], v[1] + v[3], v[2])
+
+    def own_layers(z, carry):
+        inner[z] = along_z(z, 8, 8 + height)
+        return carry
+
+    lax.fori_loop(0, depth, own_layers, 0, unroll=2)
+
     for n, (dy, dx) in enumerate(DIRS):
         @pl.when(exists(-dy, -dx))
         def _():
@@ -208,8 +217,11 @@
     def filter_chunk(chunk):
         for i in range(CH):
             z = chunk * CH + i
-            v = [dext[z + n] for n in range(5)]
-            main = along_y(five(v[0] + v[4], v[1] + v[3], v[2]))
+            main = along_y(
+                jnp.concatenate(
+                    [along_z(z, 0, 8), inner[z], along_z(z, 8 + height, ext)], axis=0
+                )
+            )
             main = jnp.where(in_rows, main, 0.0)
             back = (LANES - 4 * z) % LANES
             edge = jnp.where(
@@ -305,9 +317,10 @@
         target = lax.rem(c + k, cols_n)
         brick = jnp.int32(0)
         found = jnp.int32(0)
-        for t in range(active.shape[1]):
-            hit = jnp.logical_and(owner[0, t] == target, active[0, t] >= 0)
-            brick = jnp.where(hit, active[0, t], brick)
+        for t in range(codes.shape[1]):
+            code = codes[0, t]
+            hit = jnp.right_shift(code, 8) == target
+            brick = jnp.where(hit, jnp.bitwise_and(code, 255), brick)
             found = jnp.where(hit, 1, found)
         picks.append((brick, found))
 
@@ -331,7 +344,7 @@
             layer(chunk * CH + z)
             return inner
 
-        lax.fori_loop(0, CH, one_layer, 0, unroll=2)
+        lax.fori_loop(0, CH, one_layer, 0, unroll=4)
         start = pl.multiple_of(chunk * crows, crows)
         rows = pl.ds(start, crows)
         for k in range(1, cols_n):
@@ -427,13 +440,14 @@
     vmem = pl.BlockSpec(memory_space=pltpu.VMEM)
     hbm = pl.BlockSpec(memory_space=pltpu.HBM)
     anywhere = pl.BlockSpec(memory_space=pl.ANY)
+    codes = jnp.where(active >= 0, owner_map * 256 + active, -1)
     smoothed, received = pl.pallas_call(
         functools.partial(kernel, rows_n, cols_n),
         out_shape=(
             jax.ShapeDtypeStruct(density.shape, F32),
             jax.ShapeDtypeStruct((cols_n, PAY, LANES), F32),
         ),
-        in_specs=[hbm] * 4,
+        in_specs=[hbm] * 3,
         out_specs=(vmem, vmem),
         scratch_shapes=[
             pltpu.VMEM((depth + 4, ext, LANES), F32),
@@ -451,10 +465,10 @@
             pltpu.VMEM((local, 8, LANES), F32),
             pltpu.VMEM((2, 384 * 8, LANES), F32),
             pltpu.VMEM((cols_n, PAY, LANES), F32),
+            pltpu.VMEM(density.shape, F32),
             pltpu.SMEM(active.shape, jnp.int32),
-            pltpu.SMEM(owner_map.shape, jnp.int32),
             pltpu.SMEM(isovalues.shape, F32),
-            pltpu.SemaphoreType.DMA((4,)),
+            pltpu.SemaphoreType.DMA((3,)),
             pltpu.SemaphoreType.DMA((8,)),
             pltpu.SemaphoreType.DMA((8,)),
             pltpu.SemaphoreType.DMA((cols_n, chunks + 1)),
@@ -464,7 +478,7 @@
             collective_id=0, has_side_effects=True, vmem_limit_bytes=48 << 20
         ),
         name="halo_surface_exchange",
-    )(density, active, owner_map, isovalues)
+    )(density, codes, isovalues)
     quarter = local // 4
     capacity = (local + (cols_n - 1) * quarter + cols_n - 1) // cols_n
     cells = depth * BRICK * BRICK

time: 31.8 us -> 30.6 us (0.962)
  local copies, waits for them, and re-layouts: 3.18 us -> 1.88 us
  other arithmetic: 0 us -> 0.68 us
  Pallas kernels: 27.8 us -> 27.2 us
    unnamed x8 -> x4, local copies, waits for them, and re-layouts: 3.18 us -> 1.88 us
    select_n x0 -> x1, other arithmetic: none -> 0.68 us  [shards(): codes = jnp.where(active >= 0, owner_map * 256 + active, -1)]
    pallas_call x1, Pallas kernels: 26.6 us -> 26.1 us  [shards(): pl.pallas_call(functools.partial(kernel, rows_n, cols_n), out_shape=(jax....]
where the time goes in v2:
time: 30.6 us; the launch traced here: 30.4 us
  Pallas kernels  27.2 us (89%)
  local copies, waits for them, and re-layouts  1.88 us (6%)
  other arithmetic  0.68 us (2%)
  between operations  0.64 us (2%)
    pallas_call x1, Pallas kernels, shards(): pl.pallas_call(functools.partial(kernel, rows_n, cols_n), out_shape=(jax....  26.1 us
    unnamed x4, local copies, waits for them, and re-layouts  1.88 us
    pallas_call x1, Pallas kernels, shards(): pl.pallas_call(place, out_shape=(jax.ShapeDtypeStruct(density.shape, F32)...  1.14 us
    select_n x1, other arithmetic, shards(): codes = jnp.where(active >= 0, owner_map * 256 + active, -1)  0.68 us

profile of v2, /device:TPU:0, one launch (start us, length us, event | category | flops | bytes accessed | tf_op | source)
XLA Modules:
  0.0 30.4 jit_solution(7996566191027991914)
XLA Ops:
  0.6 0.7 %compare_select_fusion.codes_in = s32[1,8]{1,0:T(1,128)S(1)} fusion(s32[1,8]{1,0:T(1,128)} %param.5, s32[1,8]{1,0:T(1,128)} %param.6), kind=kLoop, calls=%fused_computation | loop fusion | flops 32 | bytes 96 | tf_op jit(solution)/shard_map/jit(_where)/select_n | solution.py:443
  1.3 0.0 copy-start
  1.3 1.2 %copy-done = f32[32,64,128]{2,1,0:T(8,128)S(1)} copy-done((f32[32,64,128]{2,1,0:T(8,128)S(1)}, f32[32,64,128]{2,1,0:T(8,128)}, u32[]{:S(2)}) %copy-start) | copy-done | bytes 1048600
  2.5 0.0 copy-start.1
  2.5 0.7 %copy-done.1 = f32[3]{0:T(128)S(1)} copy-done((f32[3]{0:T(128)S(1)}, f32[3]{0:T(128)}, u32[]{:S(2)}) %copy-start.1) | copy-done | bytes 36
  3.2 26.1 %halo_surface_exchange.1 = (f32[32,64,128]{2,1,0:T(8,128)S(1)}, f32[8,264,128]{2,1,0:T(8,128)S(1)}) custom-call(f32[32,64,128]{2,1,0:T(8,128)S(1)} %copy-done, s32[1,8]{1,0:T(1,128)S(1)} %compare_select_fusion.codes_in, f32[3]{0:T(128)S(1)} %copy-done.1), custom_call_target="tpu_custom_call" | custom-call | tf_op jit(solution)/shard_map/halo_surface_exchange/pallas_call | solution.py:444
  29.3 1.1 %place_slots.1 = (f32[32,64,128]{2,1,0:T(8,128)}, f32[3,256,128]{2,1,0:T(8,128)}, f32[3,1,288]{2,1,0:T(1,128)}) custom-call(f32[32,64,128]{2,1,0:T(8,128)S(1)} %get-tuple-element.8.smooth_in, f32[8,264,128]{2,1,0:T(8,128)S(1)} %get-tuple-element.9.recv), custom_call_target="tpu_custom_call" | custom-call | tf_op jit(solution)/shard_map/place_slots/pallas_call | solution.py:486
Async XLA Ops:
  1.3 1.2 %copy-start = (f32[32,64,128]{2,1,0:T(8,128)S(1)}, f32[32,64,128]{2,1,0:T(8,128)}, u32[]{:S(2)}) copy-start(f32[32,64,128]{2,1,0:T(8,128)} %dens.1) | copy-start | bytes 3145732
  2.5 0.7 %copy-start.1 = (f32[3]{0:T(128)S(1)}, f32[3]{0:T(128)}, u32[]{:S(2)}) copy-start(f32[3]{0:T(128)} %iso_in.1) | copy-start | bytes 40
